TPU v7x, 32 devices: a whole 2x2x4 slice. The times are simulated.
32 devices in a mesh: table: 4 (over y, x), fsdp: 8 (over z, core).
Axes of the slice: x: 2, y: 2, z: 4, core: 2. Of those that a mesh axis runs over, the one named last changes fastest.
Arguments:
- table_rows: bfloat16 [8, 2048, 128], P('fsdp', 'table'), may hold values from -6 to 6
- requests: int32 [8, 4, 4, 32], P('fsdp', 'table'), may hold values from -1 to 511, as said below
- bag_slots: int32 [8, 64, 26, 4], P('fsdp', 'table'), may hold values from -1 to 127, as said below
- pattern: int32 [64, 7], replicated, may hold values from 0 to 25, as said below
- tiles: bfloat16 [64, 7, 128, 128], P('table', None, 'fsdp'), may hold values from -0.1875 to 0.1875
- cotangent: bfloat16 [8, 64, 8192], P('fsdp', None, 'table'), may hold values from -6 to 6
Outputs:
- activation: bfloat16 [8, 64, 8192], P('fsdp', None, 'table')
- row_grads: float32 [8, 2048, 128], P('fsdp', 'table')
Inputs may be any that keep to these rules, and one draw needn't show every extreme that they name: Each list requests[f, o, d] holds between 8 and 32 distinct row indices followed by -1 in its remaining slots; in each group one owner's lists are all full. `bag_slots`: every entry that is not -1 names a slot that holds a row (not -1 in requests); the first entry of each bag is never -1 and -1 entries come only after all others. `pattern`: the 7 numbers of a column block are distinct.
All inputs are finite; a program needn't handle non-finite values.
Results may differ from a plain program's by a relative error of at most 0.012.
Values may be sent and summed in bfloat16 or wider, within the bound.
A program may use at most 64 MiB of HBM per device.

v0:
```python
import jax
import jax.numpy as jnp
from jax import lax
from jax.sharding import PartitionSpec as P


def local(table_rows, requests, bag_slots, pattern, tiles, cotangent):
    table_shard = table_rows[0]
    row_count = table_shard.shape[0]
    emb_width = table_shard.shape[1]
    request_list = requests[0, 0]
    peer_count = request_list.shape[0]
    slot_cap = request_list.shape[1]
    is_live = request_list >= 0
    sent_rows = jnp.take(table_shard, jnp.where(is_live, request_list, 0), axis=0)
    sent_rows = jnp.where(is_live[..., None], sent_rows, jnp.zeros_like(sent_rows))
    received = lax.all_to_all(sent_rows, "table", split_axis=0, concat_axis=0, tiled=True)
    slot_rows = received.reshape(peer_count * slot_cap, emb_width)
    bag_index = bag_slots[0]
    samples = bag_index.shape[0]
    feat_count = bag_index.shape[1]
    bag_depth = bag_index.shape[2]
    bag_live = bag_index >= 0
    values = jnp.take(slot_rows, jnp.where(bag_live, bag_index, 0).reshape(-1), axis=0)
    values = values.reshape(samples, feat_count, bag_depth, emb_width).astype(jnp.float32)
    values = jnp.where(bag_live[..., None], values, jnp.float32(0.0))
    pooled = jnp.sum(values, axis=2).astype(jnp.bfloat16)
    col_blocks = tiles.shape[0]
    per_block = tiles.shape[1]
    my_index = lax.axis_index("table")
    own_pattern = lax.dynamic_slice_in_dim(pattern, my_index * col_blocks, col_blocks, 0)
    group_rows = cotangent.shape[1]
    gathered = lax.all_gather(pooled, "table", axis=0, tiled=True)
    picked = jnp.take(gathered, own_pattern.reshape(-1), axis=1)
    picked = picked.reshape(group_rows, col_blocks, per_block * emb_width)
    full_tiles = lax.all_gather(tiles, "fsdp", axis=2, tiled=True)
    weights = full_tiles.reshape(col_blocks, per_block * emb_width, emb_width)
    pre_act = jnp.einsum("gck,ckj->gcj", picked, weights, preferred_element_type=jnp.float32)
    activation = (
        jax.nn.silu(pre_act).astype(jnp.bfloat16).reshape(1, group_rows, col_blocks * emb_width)
    )
    sigmoid_v = jax.nn.sigmoid(pre_act)
    upstream = cotangent[0].reshape(group_rows, col_blocks, emb_width).astype(jnp.float32)
    grad_pre = (upstream * sigmoid_v * (1.0 + pre_act * (1.0 - sigmoid_v))).astype(jnp.bfloat16)
    grad_picked = jnp.einsum("gcj,ckj->gck", grad_pre, weights, preferred_element_type=jnp.float32)
    grad_picked = grad_picked.reshape(group_rows, col_blocks * per_block, emb_width)
    own_flat = own_pattern.reshape(-1)
    onehot = (own_flat[:, None] == jnp.arange(feat_count, dtype=jnp.int32)[None, :]).astype(
        jnp.float32
    )
    partial_value = jnp.einsum("gme,mf->gfe", grad_picked, onehot, precision=lax.Precision.HIGHEST)
    grad_pooled = lax.psum_scatter(
        partial_value.astype(jnp.bfloat16), "table", scatter_dimension=0, tiled=True
    ).astype(jnp.float32)
    spread = jnp.broadcast_to(
        grad_pooled[:, :, None, :], (samples, feat_count, bag_depth, emb_width)
    )
    spread = jnp.where(bag_live[..., None], spread, jnp.float32(0.0)).reshape(-1, emb_width)
    segment_ids = jnp.where(bag_live, bag_index, peer_count * slot_cap).reshape(-1)
    slot_grads = jax.ops.segment_sum(spread, segment_ids, num_segments=peer_count * slot_cap + 1)
    slot_grads = slot_grads[: peer_count * slot_cap].reshape(peer_count, slot_cap, emb_width)
    returned = lax.all_to_all(
        slot_grads.astype(jnp.bfloat16), "table", split_axis=0, concat_axis=0, tiled=True
    ).astype(slot_grads.dtype)
    row_ids = jnp.where(is_live, request_list, row_count).reshape(-1)
    row_grads = jax.ops.segment_sum(
        returned.reshape(-1, emb_width), row_ids, num_segments=row_count + 1
    )
    row_grads = row_grads[:row_count].reshape(1, row_count, emb_width)
    return (activation, row_grads)


def solution(mesh):
    in_specs = (
        P("fsdp", "table", None),
        P("fsdp", "table", None, None),
        P("fsdp", "table", None, None),
        P(),
        P("table", None, "fsdp", None),
        P("fsdp", None, "table"),
    )
    out_specs = (P("fsdp", None, "table"), P("fsdp", "table", None))
    return jax.shard_map(local, mesh=mesh, in_specs=in_specs, out_specs=out_specs, check_vma=False)
```

profile of v0, /device:TPU:0, one launch (start us, length us, event | category | flops | bytes accessed | tf_op | source)
XLA Modules:
  0.0 127.8 jit_solution(9132614504227119619)
XLA Ops:
  7.2 0.7 all-gather.2.cloned.1.call-update
  7.9 0.7 compare_select_fusion.5
  8.7 0.7 gather_fusion
  9.4 0.7 bitcast_compare_fusion.1
  10.1 0.7 select_select_fusion
  10.8 5.2 %all-to-all-start = ((bf16[4,32,128]{2,1,0:T(8,128)(2,1)}), bf16[4,32,128]{2,1,0:T(8,128)(2,1)S(1)}, u32[]{:S(2)}, u32[]{:S(2)}) async-start(bf16[4,32,128]{2,1,0:T(8,128)(2,1)} %select_select_fusion), calls=%async_computation | async-start | bytes 65536 | tf_op jit(solution)/shard_map/all_to_all | solution.py:17
  16.0 0.8 compare_and_fusion.1
  16.9 1.0 copy.28
  18.1 0.8 bitcast_compare_fusion
  18.9 1.0 convert_bitcast_fusion
  20.8 3.9 %gather_fusion.1 = bf16[1664,128]{1,0:T(8,128)(2,1)S(1)} fusion(bf16[128,128]{1,0:T(8,128)(2,1)S(1)} %bitcast.59, s32[2048]{0:T(1024)S(1)} %pad_clamp_fusion), kind=kCustom, calls=%fused_computation.1 | custom fusion | bytes 858624 | tf_op jit(solution)/shard_map/jit(_take)/gather | solution.py:24
  24.7 1.3 select_reduce_fusion
  26.0 12.2 %all_gather.6 = bf16[64,26,128]{2,0,1:T(8,128)(2,1)S(1)} all-gather(bf16[16,26,128]{2,0,1:T(8,128)(2,1)S(1)} %copy.52), channel_id=1, replica_groups=mesh['table'=4,'fsdp'=8] {'table'}, dimensions={0}, use_global_device_ids=true | all-gather | bytes 532480 | tf_op jit(solution)/shard_map/all_gather | solution.py:33
  38.2 2.0 %gather_fusion.2 = bf16[112,64,128]{2,1,0:T(8,128)(2,1)} fusion(bf16[64,26,128]{2,0,1:T(8,128)(2,1)S(1)} %all_gather.6, s32[1024]{0:T(1024)S(1)} %pad_clamp_fusion.1), kind=kCustom, calls=%fused_computation.2 | custom fusion | bytes 3670464 | tf_op jit(solution)/shard_map/jit(_take)/gather | solution.py:34
  40.2 2.7 %copy.31 = bf16[64,112,128]{2,1,0:T(8,128)(2,1)S(1)} copy(bf16[64,112,128]{2,0,1:T(8,128)(2,1)} %bitcast.60) | data formatting | bytes 3670016 | tf_op jit(solution)/shard_map/jit(_take)/gather | solution.py:34
  42.9 2.8 %gather.20 = bf16[64,16,896]{2,1,0:T(8,128)(2,1)} reshape(bf16[64,112,128]{2,1,0:T(8,128)(2,1)S(1)} %copy.31) | data formatting | bytes 3670016 | tf_op jit(solution)/shard_map/jit(_take)/gather | solution.py:34
  45.7 1.7 %broadcast_select_fusion = bf16[64,16,896]{2,1,0:T(8,128)(2,1)S(1)} fusion(bf16[64,16,896]{2,1,0:T(8,128)(2,1)} %gather.20, pred[16,896]{1,0:T(8,128)(4,1)S(1)} %bitcast.69), kind=kLoop, calls=%fused_computation.8 | loop fusion | flops 917504 | bytes 3684352 | tf_op jit(solution)/shard_map/jit(_take)/select_n | solution.py:34
  47.4 8.4 %all-gather.2.cloned.1.call-done = bf16[16,7,128,128]{3,2,1,0:T(8,128)(2,1)} async-done(((bf16[16,7,16,128]{3,2,1,0:T(8,128)(2,1)}), bf16[16,7,128,128]{3,2,1,0:T(8,128)(2,1)}) %all-gather.2.cloned.1.call-update) | async-done | bytes 3670032 | tf_op jit(solution)/shard_map/all_gather | solution.py:36
  55.8 3.2 %multiply_convert_fusion = (bf16[64,16,128]{2,0,1:T(8,128)(2,1)S(1)}, f32[64,16,128]{2,0,1:T(8,128)S(1)}) fusion(bf16[16,896,128]{2,1,0:T(8,128)(2,1)} %bitcast.61, bf16[64,16,896]{2,1,0:T(8,128)(2,1)S(1)} %broadcast_select_fusion), kind=kOutput, calls=%fused_computation.19 | convolution fusion | flops 235536384 | bytes 6291456 | tf_op jit(solution)/shard_map/gck,ckj->gcj/dot_general | solution.py:38
  59.0 1.6 %convolution_bitcast_fusion = f32[64,16,896]{2,0,1:T(8,128)S(1)} fusion(bf16[16,896,128]{2,1,0:T(8,128)(2,1)S(1)} %bitcast.62, f32[64,16,128]{2,1,0:T(8,128)S(1)} %bitcast.64, f32[64,16,128]{2,0,1:T(8,128)S(1)} %get-tuple-element.11), kind=kOutput, calls=%fused_computation.5 | convolution fusion | flops 236060672 | bytes 8388608 | tf_op jit(solution)/shard_map/gcj,ckj->gck/dot_general | solution.py:45
  60.6 4.0 %copy.37 = f32[64,16,896]{2,1,0:T(8,128)} copy(f32[64,16,896]{2,0,1:T(8,128)S(1)} %convolution_bitcast_fusion) | data formatting | bytes 7340032 | tf_op jit(solution)/shard_map/gcj,ckj->gck/transpose | solution.py:45
  64.5 4.6 %reshape.204 = f32[64,112,128]{2,1,0:T(8,128)} reshape(f32[64,16,896]{2,1,0:T(8,128)} %copy.37) | data formatting | bytes 7340032 | tf_op jit(solution)/shard_map/reshape | solution.py:46
  69.1 4.3 %fusion.2 = bf16[64,26,128]{2,1,0:T(8,128)(2,1)} fusion(f32[64,112,128]{2,1,0:T(8,128)} %reshape.204, s32[112]{0:T(128)S(1)} %reshape.203), kind=kOutput, calls=%fused_computation.10 | convolution fusion | flops 286477152 | bytes 4096448 | tf_op jit(solution)/shard_map/gme,mf->gfe/dot_general | solution.py:51
  74.0 22.7 %reduce-scatter.2.cloned.1.call-done = bf16[16,26,128]{2,1,0:T(8,128)(2,1)} async-done(((bf16[64,26,128]{2,1,0:T(8,128)(2,1)}), bf16[16,26,128]{2,1,0:T(8,128)(2,1)}) %reduce-scatter.2.cloned.1.call-update) | async-done | bytes 106512 | tf_op jit(solution)/shard_map/reduce_scatter | solution.py:52
  96.6 1.0 broadcast_in_dim.104
  97.7 12.8 %scatter_custom_fusion = f32[129,128]{1,0:T(8,128)S(1)} fusion(s32[1664]{0:T(1024)S(1)} %get-tuple-element.2, f32[1664,128]{1,0:T(8,128)S(1)} %bitcast.63, f32[]{:T(128)} %constant.66.clone.1, pred[1664]{0:T(1024)(128)(4,1)S(1)} %ge.114), kind=kCustom, calls=%fused_computation.12 | custom fusion | flops 425984 | bytes 921088 | tf_op jit(solution)/shard_map/scatter-add | solution.py:60
  110.4 0.6 slice.19
  111.1 3.3 %all-to-all-start.1 = ((bf16[4,32,128]{2,1,0:T(8,128)(2,1)}), bf16[4,32,128]{2,1,0:T(8,128)(2,1)S(1)}, u32[]{:S(2)}, u32[]{:S(2)}) async-start(bf16[4,32,128]{2,1,0:T(8,128)(2,1)} %bitcast.16), calls=%async_computation.2 | async-start | bytes 65536 | tf_op jit(solution)/shard_map/all_to_all | solution.py:62
  114.5 0.8 reshape.202
  115.3 3.7 %all-to-all-done.1 = bf16[4,32,128]{2,1,0:T(8,128)(2,1)S(1)} async-done(((bf16[4,32,128]{2,1,0:T(8,128)(2,1)}), bf16[4,32,128]{2,1,0:T(8,128)(2,1)S(1)}, u32[]{:S(2)}, u32[]{:S(2)}) %all-to-all-start.1) | async-done | bytes 32800 | tf_op jit(solution)/shard_map/all_to_all | solution.py:62
  119.1 1.2 scatter_custom_fusion.1
  120.3 0.7 slice_bitcast_fusion
  (35 shorter events, 2.1 us)
Async XLA Ops:
  7.2 1.5 %copy-start = (bf16[1,512,128]{2,1,0:T(8,128)(2,1)S(1)}, bf16[1,512,128]{2,1,0:T(8,128)(2,1)}, u32[]{:S(2)}) copy-start(bf16[1,512,128]{2,1,0:T(8,128)(2,1)} %param.6) | copy-start | bytes 393220
  7.2 48.7 %all-gather.2.cloned.1.call-start = ((), (), s32[]{:S(2)}) async-start(), calls=%async_computation.3 | async-start | bytes 4128768 | tf_op jit(solution)/shard_map/all_gather | solution.py:36
  10.8 10.0 %all-to-all-start = ((bf16[4,32,128]{2,1,0:T(8,128)(2,1)}), bf16[4,32,128]{2,1,0:T(8,128)(2,1)S(1)}, u32[]{:S(2)}, u32[]{:S(2)}) async-start(bf16[4,32,128]{2,1,0:T(8,128)(2,1)} %select_select_fusion), calls=%async_computation | async-start | bytes 65536 | tf_op jit(solution)/shard_map/all_to_all | solution.py:17
  16.0 80.7 %reduce-scatter.2.cloned.1.call-start = ((), (), s32[]{:S(2)}) async-start(), calls=%async_computation.4 | async-start | bytes 655360 | tf_op jit(solution)/shard_map/reduce_scatter | solution.py:52
  55.8 3.2 %copy-start.1 = (bf16[16,7,128,128]{3,2,1,0:T(8,128)(2,1)S(1)}, bf16[16,7,128,128]{3,2,1,0:T(8,128)(2,1)}, u32[]{:S(2)}) copy-start(bf16[16,7,128,128]{3,2,1,0:T(8,128)(2,1)} %all-gather.2.cloned.1.call-done) | copy-start | bytes 11010052
  69.1 4.3 %copy-start.3 = (s32[1,1,4,32]{3,2,1,0:T(4,128)S(1)}, s32[1,1,4,32]{3,2,1,0:T(4,128)}, u32[]{:S(2)}) copy-start(s32[1,1,4,32]{3,2,1,0:T(4,128)} %param.7) | copy-start | bytes 1540
  69.1 4.4 %copy-start.2 = (s32[1,16,26,4]{2,3,1,0:T(4,128)S(1)}, s32[1,16,26,4]{2,3,1,0:T(4,128)}, u32[]{:S(2)}) copy-start(s32[1,16,26,4]{2,3,1,0:T(4,128)} %param.8) | copy-start | bytes 19972
  111.1 8.0 %all-to-all-start.1 = ((bf16[4,32,128]{2,1,0:T(8,128)(2,1)}), bf16[4,32,128]{2,1,0:T(8,128)(2,1)S(1)}, u32[]{:S(2)}, u32[]{:S(2)}) async-start(bf16[4,32,128]{2,1,0:T(8,128)(2,1)} %bitcast.16), calls=%async_computation.2 | async-start | bytes 65536 | tf_op jit(solution)/shard_map/all_to_all | solution.py:62
Sparse Core Ops, SparseCore 0:
  9.6 46.1 all-gather.1
  73.6 23.0 reduce-scatter.1
where the time goes:
time: 128 us
  waiting for transfers between devices  35.5 us (28%)
  local copies, waits for them, and re-layouts  26.8 us (21%)
  other arithmetic  21.7 us (17%)
  between operations  14.2 us (11%)
  blocking collectives  12.2 us (10%)
  matrix products  9.03 us (7%)
  starting transfers between devices  8.47 us (7%)
    reduce_scatter x1, waiting for transfers between devices, local(): lax.psum_scatter(partial_value.astype(jnp.bfloat16), 'table', scatter_dim...  22.7 us
    scatter-add x1, other arithmetic, local(): jax.ops.segment_sum(spread, segment_ids, num_segments=peer_count * slot_c...  12.8 us
    all_gather x1, blocking collectives, local(): gathered = lax.all_gather(pooled, 'table', axis=0, tiled=True)  12.2 us
    all_gather x1, waiting for transfers between devices, local(): full_tiles = lax.all_gather(tiles, 'fsdp', axis=2, tiled=True)  8.41 us
    gather x3, local copies, waits for them, and re-layouts, local(): picked = jnp.take(gathered, own_pattern.reshape(-1), axis=1)  7.53 us
    all_to_all x1, starting transfers between devices, local(): lax.all_to_all(sent_rows, 'table', split_axis=0, concat_axis=0, tiled=True)  5.16 us
    reshape x1, local copies, waits for them, and re-layouts, local(): grad_picked.reshape(group_rows, col_blocks * per_block, emb_width)  4.58 us
    dot_general x1, matrix products, local(): jnp.einsum('gme,mf->gfe', grad_picked, onehot, precision=lax.Precision.HI...  4.32 us
  transfers between devices with their start and end apart: 4, of which 3 were waited for; matrix products, arithmetic and copies ran while one was open for 18% of the time, Pallas kernels for 0%

commit v1 on v0

--- a/solution.py
+++ b/solution.py
@@ -1,7 +1,18 @@
+import functools
+
 import jax
 import jax.numpy as jnp
 from jax import lax
+from jax.experimental import pallas as pl
+from jax.experimental.pallas import tpu as pltpu
 from jax.sharding import PartitionSpec as P
+
+MESH = pl.DeviceIdType.MESH
+F32 = jnp.float32
+BF16 = jnp.bfloat16
+TILE_ROWS = 16
+VMEM_LIMIT = 48 * 1024 * 1024
+CHUNKS = 4
 
 
 def local(table_rows, requests, bag_slots, pattern, tiles, cotangent):
@@ -70,7 +81,377 @@
     return (activation, row_grads)
 
 
+def contract(lhs, rhs, lhs_dim, rhs_dim):
+    return lax.dot_general(
+        lhs, rhs, (((lhs_dim,), (rhs_dim,)), ((), ())), preferred_element_type=F32
+    )
+
+
+def body(
+    n_table,
+    n_fsdp,
+    chunks,
+    table_ref,
+    req_ref,
+    bag_ref,
+    pattern_ref,
+    tiles_ref,
+    cot_ref,
+    act_ref,
+    rows_ref,
+    w,
+    cot,
+    act,
+    req_row,
+    bag_rows,
+    pick,
+    counts,
+    sent,
+    received,
+    spread,
+    pooled,
+    products,
+    total,
+    part,
+    parts_in,
+    back,
+    back_in,
+    plan,
+    plan_s,
+    local_sem,
+    w_send,
+    w_recv,
+    t_send,
+    t_recv,
+):
+    col_blocks, per_block, tile_rows, emb = tiles_ref.shape
+    step = col_blocks // chunks
+    lines = n_fsdp // 2
+    samples, depth, feats = bag_ref.shape[1:]
+    slot_cap = req_ref.shape[3]
+    slots = n_table * slot_cap
+    group = cot_ref.shape[1]
+    row_count = table_ref.shape[1]
+    pad = bag_rows.shape[2] // (samples // bag_rows.shape[0])
+
+    me = lax.axis_index("table")
+    mine = lax.axis_index("fsdp")
+    z = mine // 2
+    core = mine % 2
+    sibling = 2 * z + 1 - core
+
+    barrier = pltpu.get_barrier_semaphore()
+    for d in range(1, n_table):
+        pl.semaphore_signal(
+            barrier, inc=1, device_id={"table": lax.rem(me + d, n_table)}, device_id_type=MESH
+        )
+    pl.semaphore_signal(barrier, inc=1, device_id={"fsdp": sibling}, device_id_type=MESH)
+
+    @pl.when(z > 0)
+    def _():
+        pl.semaphore_signal(barrier, inc=1, device_id={"fsdp": mine - 2}, device_id_type=MESH)
+
+    @pl.when(z < lines - 1)
+    def _():
+        pl.semaphore_signal(barrier, inc=1, device_id={"fsdp": mine + 2}, device_id_type=MESH)
+
+    own_tiles = pltpu.make_async_copy(
+        tiles_ref,
+        w.at[:, :, pl.ds(pl.multiple_of(mine * tile_rows, tile_rows), tile_rows), :],
+        local_sem.at[0],
+    )
+    own_tiles.start()
+    own_cot = pltpu.make_async_copy(cot_ref.at[0], cot, local_sem.at[1])
+    own_cot.start()
+
+    neighbours = jnp.where(z > 0, 1, 0) + jnp.where(z < lines - 1, 1, 0)
+    pl.semaphore_wait(barrier, n_table + neighbours)
+
+    def slot(chunk, source):
+        at = pl.multiple_of(source * tile_rows, tile_rows)
+        return w.at[pl.ds(chunk * step, step), :, pl.ds(at, tile_rows), :]
+
+    def hop(way, chunk, line, target, own=False):
+        source = 2 * line + core
+        src = tiles_ref.at[pl.ds(chunk * step, step)] if own else slot(chunk, source)
+        return pltpu.make_async_remote_copy(
+            src_ref=src,
+            dst_ref=slot(chunk, source),
+            send_sem=w_send.at[way, chunk, line],
+            recv_sem=w_recv.at[chunk, source],
+            device_id={"fsdp": target},
+            device_id_type=MESH,
+        )
+
+    def landed(chunk, source):
+        pltpu.make_async_remote_copy(
+            src_ref=slot(chunk, source),
+            dst_ref=slot(chunk, source),
+            send_sem=w_send.at[2, chunk, z],
+            recv_sem=w_recv.at[chunk, source],
+            device_id={"fsdp": sibling},
+            device_id_type=MESH,
+        ).wait_recv()
+
+    def send_own(chunk, carry):
+        @pl.when(z < lines - 1)
+        def _():
+            hop(0, chunk, z, mine + 2, True).start()
+
+        @pl.when(z > 0)
+        def _():
+            hop(1, chunk, z, mine - 2, True).start()
+
+        return carry
+
+    lax.fori_loop(0, chunks, send_own, 0)
+
+    def send_own_core(chunk, carry):
+        hop(2, chunk, z, sibling, True).start()
+        return carry
+
+    lax.fori_loop(0, chunks, send_own_core, 0)
+
+    def exchange(phase, source_of, target):
+        copies = []
+        for d in range(1, n_table):
+            peer = lax.rem(me + d, n_table)
+            copy = pltpu.make_async_remote_copy(
+                src_ref=source_of(peer),
+                dst_ref=target,
+                send_sem=t_send.at[phase, d],
+                recv_sem=t_recv.at[phase, d],
+                device_id={"table": peer},
+                device_id_type=MESH,
+            )
+            copy.start()
+            copies.append(copy)
+        return copies
+
+    for d in range(n_table):
+        req_row[:, d * slot_cap : (d + 1) * slot_cap] = req_ref[0, 0, d : d + 1, :]
+    row_ids = lax.broadcasted_iota(jnp.int32, (row_count, slots), 0)
+    pick[...] = jnp.where(row_ids == req_row[...], 1.0, 0.0).astype(BF16)
+    sent[...] = (
+        contract(pick[...], table_ref[0], 0, 0).astype(BF16).reshape(n_table, slot_cap, emb)
+    )
+    first = exchange(0, lambda peer: sent.at[peer], received.at[me])
+    received[me] = sent[me]
+
+    bag_rows[...] = jnp.full(bag_rows.shape, -1, jnp.int32)
+    per_row = samples // bag_rows.shape[0]
+    for s in range(samples):
+        at = (s % per_row) * pad
+        bag_rows[s // per_row, :, at : at + feats] = bag_ref[0, s]
+    width = per_row * pad
+    slot_ids = lax.broadcasted_iota(jnp.int32, (slots, width), 0)
+    for g in range(bag_rows.shape[0]):
+        rows = bag_rows[g]
+        found = jnp.zeros((slots, width), F32)
+        for k in range(depth):
+            found = found + jnp.where(slot_ids == rows[k : k + 1, :], 1.0, 0.0)
+        counts[:, g * width : (g + 1) * width] = found.astype(BF16)
+
+    plan[...] = jnp.zeros(plan.shape, jnp.int32)
+    feat_ids = lax.broadcasted_iota(jnp.int32, (plan.shape[0] - 8, pattern_ref.shape[1]), 0)
+    inverse = jnp.full(feat_ids.shape, per_block, jnp.int32)
+    for i in range(per_block):
+        inverse = jnp.where(feat_ids == pattern_ref[i : i + 1, :], i, inverse)
+    plan[0 : plan.shape[0] - 8, 0 : pattern_ref.shape[1]] = inverse
+    plan[plan.shape[0] - 8 : plan.shape[0] - 8 + per_block, 0 : pattern_ref.shape[1]] = pattern_ref[
+        ...
+    ]
+    to_scalar = pltpu.make_async_copy(plan, plan_s, local_sem.at[2])
+    to_scalar.start()
+    products[...] = jnp.zeros(products.shape, F32)
+
+    for copy in first:
+        copy.wait_recv()
+    spread[...] = contract(counts[...], received[...].reshape(slots, emb), 0, 0)
+    at_me = pl.ds(pl.multiple_of(me * samples, samples), samples)
+    for j in range(feats):
+        pooled[j, at_me, :] = spread[pl.ds(j, samples, stride=pad), :].astype(BF16)
+    second = exchange(1, lambda peer: pooled.at[:, at_me, :], pooled.at[:, at_me, :])
+    to_scalar.wait()
+    own_cot.wait()
+    own_tiles.wait()
+
+    def arrive(chunk, distance):
+        @pl.when(z >= distance)
+        def _():
+            landed(chunk, mine - 2 * distance)
+
+            @pl.when(z < lines - 1)
+            def _():
+                hop(0, chunk, z - distance, mine + 2).start()
+
+            hop(2, chunk, z - distance, sibling).start()
+
+        @pl.when(z + distance < lines)
+        def _():
+            landed(chunk, mine + 2 * distance)
+
+            @pl.when(z > 0)
+            def _():
+                hop(1, chunk, z + distance, mine - 2).start()
+
+            hop(2, chunk, z + distance, sibling).start()
+
+    for distance in range(1, lines - 1):
+        lax.fori_loop(
+            0, chunks, lambda chunk, carry, distance=distance: (arrive(chunk, distance), carry)[1], 0
+        )
+    for copy in second:
+        copy.wait_recv()
+
+    def work(chunk, carry):
+        arrive(chunk, lines - 1)
+        for line in range(lines):
+            landed(chunk, 2 * line + 1 - core)
+        for b in range(step):
+            n = chunk * step + b
+            picked = jnp.concatenate(
+                [
+                    pooled[plan_s[plan.shape[0] - 8 + i, me * col_blocks + n]]
+                    for i in range(per_block)
+                ],
+                axis=1,
+            )
+            weights = w[n].reshape(per_block * emb, emb)
+            pre = contract(picked, weights, 1, 0)
+            sig = jax.nn.sigmoid(pre)
+            columns = pl.ds(pl.multiple_of(n * emb, emb), emb)
+            act[:, columns] = (pre * sig).astype(BF16)
+            up = cot[:, columns].astype(F32)
+            grad = (up * sig * (1.0 + pre * (1.0 - sig))).astype(BF16)
+            back_rows = contract(grad, weights, 1, 1)
+            for i in range(per_block):
+                products[b, i] = back_rows[:, i * emb : (i + 1) * emb]
+
+        def add(j, c):
+            value = products[0, plan_s[j, me * col_blocks + chunk * step]]
+            for b in range(1, step):
+                value = value + products[b, plan_s[j, me * col_blocks + chunk * step + b]]
+            total[j] = jnp.where(chunk == 0, value, total[j] + value)
+            return c
+
+        lax.fori_loop(0, feats, add, 0, unroll=2)
+        return carry
+
+    total[...] = jnp.zeros(total.shape, F32)
+    lax.fori_loop(0, chunks, work, 0)
+    act_out = pltpu.make_async_copy(act, act_ref.at[0], local_sem.at[3])
+    act_out.start()
+
+    part[...] = total[...].astype(BF16)
+    third = exchange(
+        2,
+        lambda peer: part.at[:, pl.ds(pl.multiple_of(peer * samples, samples), samples), :],
+        parts_in.at[me],
+    )
+    parts_in[me] = part[:, at_me, :]
+    spread[...] = jnp.zeros(spread.shape, F32)
+    for copy in third:
+        copy.wait_recv()
+    for j in range(feats):
+        value = parts_in[0, j].astype(F32)
+        for d in range(1, n_table):
+            value = value + parts_in[d, j].astype(F32)
+        spread[pl.ds(j, samples, stride=pad), :] = value
+    grads = spread[...]
+    high = grads.astype(BF16)
+    low = (grads - high.astype(F32)).astype(BF16)
+    slot_grads = contract(counts[...], high, 1, 0) + contract(counts[...], low, 1, 0)
+    back[...] = slot_grads.astype(BF16).reshape(n_table, slot_cap, emb)
+    fourth = exchange(3, lambda peer: back.at[peer], back_in.at[me])
+    back_in[me] = back[me]
+    for copy in fourth:
+        copy.wait_recv()
+    rows_ref[0] = contract(pick[...], back_in[...].reshape(slots, emb), 1, 0)
+
+    for copies in (first, second, third, fourth):
+        for copy in copies:
+            copy.wait_send()
+
+    def sent_all(chunk, carry):
+        for line in range(lines):
+            hop(2, chunk, line, sibling).wait_send()
+
+            @pl.when((line <= z) & (z < lines - 1))
+            def _():
+                hop(0, chunk, line, mine + 2).wait_send()
+
+            @pl.when((line >= z) & (z > 0))
+            def _():
+                hop(1, chunk, line, mine - 2).wait_send()
+
+        return carry
+
+    lax.fori_loop(0, chunks, sent_all, 0)
+    act_out.wait()
+
+
+def fused(n_table, n_fsdp, chunks, table_rows, requests, bag_slots, pattern, tiles, cotangent):
+    col_blocks, per_block, tile_rows, emb = tiles.shape
+    group = cotangent.shape[1]
+    row_count = table_rows.shape[1]
+    samples, feats, depth = bag_slots.shape[1:]
+    slot_cap = requests.shape[3]
+    slots = n_table * slot_cap
+    lines = n_fsdp // 2
+    pad = 32
+    per_row = 128 // pad
+    plan_rows = pad + 8
+    vmem, anywhere = pl.BlockSpec(memory_space=pltpu.VMEM), pl.BlockSpec(memory_space=pl.ANY)
+    return pl.pallas_call(
+        functools.partial(body, n_table, n_fsdp, chunks),
+        out_shape=(
+            jax.ShapeDtypeStruct((1, group, col_blocks * emb), BF16),
+            jax.ShapeDtypeStruct((1, row_count, emb), F32),
+        ),
+        in_specs=[vmem, vmem, vmem, vmem, anywhere, anywhere],
+        out_specs=(anywhere, vmem),
+        scratch_shapes=[
+            pltpu.VMEM((col_blocks, per_block, tile_rows * n_fsdp, emb), BF16),
+            pltpu.VMEM((group, col_blocks * emb), BF16),
+            pltpu.VMEM((group, col_blocks * emb), BF16),
+            pltpu.VMEM((1, slots), jnp.int32),
+            pltpu.VMEM((samples // per_row, depth, per_row * pad), jnp.int32),
+            pltpu.VMEM((row_count, slots), BF16),
+            pltpu.VMEM((slots, samples * pad), BF16),
+            pltpu.VMEM((n_table, slot_cap, emb), BF16),
+            pltpu.VMEM((n_table, slot_cap, emb), BF16),
+            pltpu.VMEM((samples * pad, emb), F32),
+            pltpu.VMEM((feats, group, emb), BF16),
+            pltpu.VMEM((col_blocks // chunks, per_block + 1, group, emb), F32),
+            pltpu.VMEM((feats, group, emb), F32),
+            pltpu.VMEM((feats, group, emb), BF16),
+            pltpu.VMEM((n_table, feats, samples, emb), BF16),
+            pltpu.VMEM((n_table, slot_cap, emb), BF16),
+            pltpu.VMEM((n_table, slot_cap, emb), BF16),
+            pltpu.VMEM((plan_rows, 128), jnp.int32),
+            pltpu.SMEM((plan_rows, 128), jnp.int32),
+            pltpu.SemaphoreType.DMA((4,)),
+            pltpu.SemaphoreType.DMA((3, chunks, lines)),
+            pltpu.SemaphoreType.DMA((chunks, n_fsdp)),
+            pltpu.SemaphoreType.DMA((4, n_table)),
+            pltpu.SemaphoreType.DMA((4, n_table)),
+        ],
+        compiler_params=pltpu.CompilerParams(
+            collective_id=0, has_side_effects=True, vmem_limit_bytes=VMEM_LIMIT
+        ),
+    )(
+        table_rows,
+        requests,
+        jnp.swapaxes(bag_slots, 2, 3),
+        pattern.T,
+        tiles,
+        cotangent,
+    )
+
+
 def solution(mesh):
+    n_table, n_fsdp = mesh.shape["table"], mesh.shape["fsdp"]
     in_specs = (
         P("fsdp", "table", None),
         P("fsdp", "table", None, None),
@@ -80,4 +461,23 @@
         P("fsdp", None, "table"),
     )
     out_specs = (P("fsdp", None, "table"), P("fsdp", "table", None))
-    return jax.shard_map(local, mesh=mesh, in_specs=in_specs, out_specs=out_specs, check_vma=False)
+
+    def program(table_rows, requests, bag_slots, pattern, tiles, cotangent):
+        col_blocks, _, tile_rows, emb = tiles.shape
+        samples, feats = bag_slots.shape[1:3]
+        whole = (
+            tile_rows % TILE_ROWS == 0
+            and samples % TILE_ROWS == 0
+            and emb == 128
+            and n_table * requests.shape[3] == 128
+            and feats <= 32
+            and n_fsdp % 2 == 0
+            and col_blocks % CHUNKS == 0
+        )
+        if whole:
+            run = functools.partial(fused, n_table, n_fsdp, CHUNKS)
+        else:
+            run = local
+        return run(table_rows, requests, bag_slots, pattern, tiles, cotangent)
+
+    return jax.shard_map(program, mesh=mesh, in_specs=in_specs, out_specs=out_specs, check_vma=False)

time: 128 us -> 58.4 us (0.46)
  Pallas kernels: 0 us -> 51 us
  waiting for transfers between devices: 35.5 us -> 0 us
  other arithmetic: 21.7 us -> 0 us
  local copies, waits for them, and re-layouts: 26.8 us -> 6.4 us
  between operations: 14.2 us -> 0.65 us
  blocking collectives: 12.2 us -> 0 us
  matrix products: 9.03 us -> 0 us
  starting transfers between devices: 8.47 us -> 0 us
    pallas_call x0 -> x1, Pallas kernels: none -> 51 us  [fused(): pl.pallas_call(functools.partial(body, n_table, n_fsdp, chunks), out_shap...]
    reduce_scatter x1 -> x0, waiting for transfers between devices: 22.7 us -> none  [local(): lax.psum_scatter(partial_value.astype(jnp.bfloat16), 'table', scatter_dim...]
    scatter-add x2 -> x0, other arithmetic: 14 us -> none  [the longest x1 12.8 us: local(): jax.ops.segment_sum(spread, segment_ids, num_segments=peer_count * slot_c...]
    all_gather x1 -> x0, blocking collectives: 12.2 us -> none  [local(): gathered = lax.all_gather(pooled, 'table', axis=0, tiled=True)]
    gather x5 -> x0, local copies, waits for them, and re-layouts: 12.1 us -> none  [the longest x3 7.53 us: local(): picked = jnp.take(gathered, own_pattern.reshape(-1), axis=1)]
    dot_general x3 -> x0, matrix products: 9.03 us -> none  [the longest x1 4.32 us: local(): jnp.einsum('gme,mf->gfe', grad_picked, onehot, precision=lax.Precision.HI...]
    all_to_all x2 -> x0, starting transfers between devices: 8.43 us -> none  [the longest x1 5.16 us: local(): lax.all_to_all(sent_rows, 'table', split_axis=0, concat_axis=0, tiled=True)]
    all_gather x1 -> x0, waiting for transfers between devices: 8.41 us -> none  [local(): full_tiles = lax.all_gather(tiles, 'fsdp', axis=2, tiled=True)]
  transfers between devices with their start and end apart: 4 -> 0, of which waited for: 3 -> 0; matrix products, arithmetic and copies ran while one was open for 18% -> 0% of each run, Pallas kernels for 0% -> 0%
where the time goes in v1:
time: 58.4 us; the launch traced here: 58 us
  Pallas kernels  51 us (87%)
  local copies, waits for them, and re-layouts  6.4 us (11%)
  between operations  0.65 us (1%)
    pallas_call x1, Pallas kernels, fused(): pl.pallas_call(functools.partial(body, n_table, n_fsdp, chunks), out_shap...  51 us
    unnamed x14, local copies, waits for them, and re-layouts  6.4 us

profile of v1, /device:TPU:0, one launch (start us, length us, event | category | flops | bytes accessed | tf_op | source)
XLA Modules:
  0.0 58.0 jit_solution(3785646803986882531)
XLA Ops:
  0.6 0.0 copy-start.5
  0.6 0.7 %copy-done.5 = s32[1,1,4,32]{3,2,1,0:T(4,128)S(1)} copy-done((s32[1,1,4,32]{3,2,1,0:T(4,128)S(1)}, s32[1,1,4,32]{3,2,1,0:T(4,128)}, u32[]{:S(2)}) %copy-start.5) | copy-done | bytes 536
  1.3 0.0 copy-start
  1.3 1.0 %copy-done = bf16[16,7,16,128]{3,2,1,0:T(8,128)(2,1)S(1)} copy-done((bf16[16,7,16,128]{3,2,1,0:T(8,128)(2,1)S(1)}, bf16[16,7,16,128]{3,2,1,0:T(8,128)(2,1)}, u32[]{:S(2)}) %copy-start) | copy-done | bytes 458776
  2.3 0.0 copy-start.1
  2.3 0.9 %copy-done.1 = bf16[1,64,2048]{2,1,0:T(8,128)(2,1)S(1)} copy-done((bf16[1,64,2048]{2,1,0:T(8,128)(2,1)S(1)}, bf16[1,64,2048]{2,1,0:T(8,128)(2,1)}, u32[]{:S(2)}) %copy-start.1) | copy-done | bytes 262168
  3.3 0.0 copy-start.2
  3.3 0.9 %copy-done.2 = bf16[1,512,128]{2,1,0:T(8,128)(2,1)S(1)} copy-done((bf16[1,512,128]{2,1,0:T(8,128)(2,1)S(1)}, bf16[1,512,128]{2,1,0:T(8,128)(2,1)}, u32[]{:S(2)}) %copy-start.2) | copy-done | bytes 131096
  4.2 0.0 copy-start.3
  4.2 0.8 %copy-done.3 = s32[1,16,26,4]{2,3,1,0:T(4,128)S(1)} copy-done((s32[1,16,26,4]{2,3,1,0:T(4,128)S(1)}, s32[1,16,26,4]{2,3,1,0:T(4,128)}, u32[]{:S(2)}) %copy-start.3) | copy-done | bytes 6680
  4.9 0.0 copy-start.4
  4.9 0.7 %copy-done.4 = s32[64,7]{0,1:T(8,128)S(1)} copy-done((s32[64,7]{0,1:T(8,128)S(1)}, s32[64,7]{0,1:T(8,128)}, u32[]{:S(2)}) %copy-start.4) | copy-done | bytes 1816
  5.6 51.0 %shard_map.77 = (bf16[1,64,2048]{2,1,0:T(8,128)(2,1)S(1)}, f32[1,512,128]{2,1,0:T(8,128)S(1)}) custom-call(bf16[1,512,128]{2,1,0:T(8,128)(2,1)S(1)} %copy-done.2, s32[1,1,4,32]{3,2,1,0:T(4,128)S(1)} %copy-done.5, s32[1,16,4,26]{3,2,1,0:T(4,128)S(1)} %bitcast.2, s32[7,64]{1,0:T(8,128)S(1)} %bitcast.3, bf16[16,7,16,128]{3,2,1,0:T(8,128)(2,1)S(1)} %copy-done, ...), custom_call_target="tpu_custom_call" | custom-call | tf_op jit(solution)/shard_map/pallas_call | solution.py:406
  56.6 0.7 %copy.10 = bf16[1,64,2048]{2,1,0:T(8,128)(2,1)} copy(bf16[1,64,2048]{2,1,0:T(8,128)(2,1)S(1)} %get-tuple-element.4) | data formatting | bytes 524288
  57.3 0.7 %copy.11 = f32[1,512,128]{2,1,0:T(8,128)} copy(f32[1,512,128]{2,1,0:T(8,128)S(1)} %get-tuple-element.5) | data formatting | bytes 524288
Async XLA Ops:
  0.6 0.7 %copy-start.5 = (s32[1,1,4,32]{3,2,1,0:T(4,128)S(1)}, s32[1,1,4,32]{3,2,1,0:T(4,128)}, u32[]{:S(2)}) copy-start(s32[1,1,4,32]{3,2,1,0:T(4,128)} %req_ref.1) | copy-start | bytes 1540
  1.3 1.0 %copy-start = (bf16[16,7,16,128]{3,2,1,0:T(8,128)(2,1)S(1)}, bf16[16,7,16,128]{3,2,1,0:T(8,128)(2,1)}, u32[]{:S(2)}) copy-start(bf16[16,7,16,128]{3,2,1,0:T(8,128)(2,1)} %tiles_ref.1) | copy-start | bytes 1376260
  2.3 0.9 %copy-start.1 = (bf16[1,64,2048]{2,1,0:T(8,128)(2,1)S(1)}, bf16[1,64,2048]{2,1,0:T(8,128)(2,1)}, u32[]{:S(2)}) copy-start(bf16[1,64,2048]{2,1,0:T(8,128)(2,1)} %cot_ref.1) | copy-start | bytes 786436
  3.3 0.9 %copy-start.2 = (bf16[1,512,128]{2,1,0:T(8,128)(2,1)S(1)}, bf16[1,512,128]{2,1,0:T(8,128)(2,1)}, u32[]{:S(2)}) copy-start(bf16[1,512,128]{2,1,0:T(8,128)(2,1)} %table_ref.1) | copy-start | bytes 393220
  4.2 0.8 %copy-start.3 = (s32[1,16,26,4]{2,3,1,0:T(4,128)S(1)}, s32[1,16,26,4]{2,3,1,0:T(4,128)}, u32[]{:S(2)}) copy-start(s32[1,16,26,4]{2,3,1,0:T(4,128)} %param.8) | copy-start | bytes 19972
  4.9 0.7 %copy-start.4 = (s32[64,7]{0,1:T(8,128)S(1)}, s32[64,7]{0,1:T(8,128)}, u32[]{:S(2)}) copy-start(s32[64,7]{0,1:T(8,128)} %param.9) | copy-start | bytes 5380

commit v2 on v1

--- a/solution.py
+++ b/solution.py
@@ -11,7 +11,7 @@
 F32 = jnp.float32
 BF16 = jnp.bfloat16
 TILE_ROWS = 16
-VMEM_LIMIT = 48 * 1024 * 1024
+VMEM_LIMIT = 64 * 1024 * 1024
 CHUNKS = 4
 
 
@@ -91,14 +91,18 @@
     n_table,
     n_fsdp,
     chunks,
+    table_in,
+    req_in,
+    bag_in,
+    pattern_in,
+    tiles_ref,
+    cot_ref,
+    act_ref,
+    rows_ref,
     table_ref,
     req_ref,
     bag_ref,
     pattern_ref,
-    tiles_ref,
-    cot_ref,
-    act_ref,
-    rows_ref,
     w,
     cot,
     act,
@@ -106,19 +110,17 @@
     bag_rows,
     pick,
     counts,
-    sent,
     received,
+    values,
     spread,
     pooled,
     products,
-    total,
-    part,
-    parts_in,
     back,
     back_in,
     plan,
     plan_s,
     local_sem,
+    load_sem,
     w_send,
     w_recv,
     t_send,
@@ -132,7 +134,7 @@
     slots = n_table * slot_cap
     group = cot_ref.shape[1]
     row_count = table_ref.shape[1]
-    pad = bag_rows.shape[2] // (samples // bag_rows.shape[0])
+    pad = bag_rows.shape[3] // (samples // bag_rows.shape[1])
 
     me = lax.axis_index("table")
     mine = lax.axis_index("fsdp")
@@ -140,6 +142,17 @@
     core = mine % 2
     sibling = 2 * z + 1 - core
 
+    loads = [
+        pltpu.make_async_copy(source, target, load_sem.at[i])
+        for i, (source, target) in enumerate(
+            (
+                (req_in, req_ref),
+                (table_in, table_ref),
+                (bag_in, bag_ref),
+                (pattern_in, pattern_ref),
+            )
+        )
+    ]
     barrier = pltpu.get_barrier_semaphore()
     for d in range(1, n_table):
         pl.semaphore_signal(
@@ -155,12 +168,13 @@
     def _():
         pl.semaphore_signal(barrier, inc=1, device_id={"fsdp": mine + 2}, device_id_type=MESH)
 
+    for load in loads:
+        load.start()
     own_tiles = pltpu.make_async_copy(
         tiles_ref,
         w.at[:, :, pl.ds(pl.multiple_of(mine * tile_rows, tile_rows), tile_rows), :],
         local_sem.at[0],
     )
-    own_tiles.start()
     own_cot = pltpu.make_async_copy(cot_ref.at[0], cot, local_sem.at[1])
     own_cot.start()
 
@@ -228,29 +242,27 @@
             copies.append(copy)
         return copies
 
+    own_tiles.start()
+    loads[0].wait()
     for d in range(n_table):
         req_row[:, d * slot_cap : (d + 1) * slot_cap] = req_ref[0, 0, d : d + 1, :]
     row_ids = lax.broadcasted_iota(jnp.int32, (row_count, slots), 0)
     pick[...] = jnp.where(row_ids == req_row[...], 1.0, 0.0).astype(BF16)
-    sent[...] = (
+    loads[1].wait()
+    received[me] = (
         contract(pick[...], table_ref[0], 0, 0).astype(BF16).reshape(n_table, slot_cap, emb)
     )
-    first = exchange(0, lambda peer: sent.at[peer], received.at[me])
-    received[me] = sent[me]
-
-    bag_rows[...] = jnp.full(bag_rows.shape, -1, jnp.int32)
-    per_row = samples // bag_rows.shape[0]
+    first = exchange(0, lambda peer: received.at[me], received.at[me])
+    loads[2].wait()
+    loads[3].wait()
+    quads = bag_rows.shape[1]
+    per_row = samples // quads
+    width = per_row * pad
+    bag_rows[me] = jnp.full(bag_rows.shape[1:], -1, jnp.int32)
     for s in range(samples):
         at = (s % per_row) * pad
-        bag_rows[s // per_row, :, at : at + feats] = bag_ref[0, s]
-    width = per_row * pad
-    slot_ids = lax.broadcasted_iota(jnp.int32, (slots, width), 0)
-    for g in range(bag_rows.shape[0]):
-        rows = bag_rows[g]
-        found = jnp.zeros((slots, width), F32)
-        for k in range(depth):
-            found = found + jnp.where(slot_ids == rows[k : k + 1, :], 1.0, 0.0)
-        counts[:, g * width : (g + 1) * width] = found.astype(BF16)
+        bag_rows[me, s // per_row, :, at : at + feats] = bag_ref[0, s]
+    second = exchange(1, lambda peer: bag_rows.at[me], bag_rows.at[me])
 
     plan[...] = jnp.zeros(plan.shape, jnp.int32)
     feat_ids = lax.broadcasted_iota(jnp.int32, (plan.shape[0] - 8, pattern_ref.shape[1]), 0)
@@ -263,15 +275,35 @@
     ]
     to_scalar = pltpu.make_async_copy(plan, plan_s, local_sem.at[2])
     to_scalar.start()
-    products[...] = jnp.zeros(products.shape, F32)
-
+    products[:, per_block] = jnp.zeros((step, group, emb), F32)
+    spread[...] = jnp.zeros(spread.shape, F32)
+
+    for copy in second:
+        copy.wait_recv()
+    slot_ids = lax.broadcasted_iota(jnp.int32, (slots, width), 0)
+
+    def count(d, carry):
+        for g in range(quads):
+            rows = bag_rows[d, g]
+            found = jnp.zeros((slots, width), F32)
+            for k in range(depth):
+                found = found + jnp.where(slot_ids == rows[k : k + 1, :], 1.0, 0.0)
+            counts[d, :, g * width : (g + 1) * width] = found.astype(BF16)
+        return carry
+
+    lax.fori_loop(0, n_table, count, 0)
     for copy in first:
         copy.wait_recv()
-    spread[...] = contract(counts[...], received[...].reshape(slots, emb), 0, 0)
-    at_me = pl.ds(pl.multiple_of(me * samples, samples), samples)
-    for j in range(feats):
-        pooled[j, at_me, :] = spread[pl.ds(j, samples, stride=pad), :].astype(BF16)
-    second = exchange(1, lambda peer: pooled.at[:, at_me, :], pooled.at[:, at_me, :])
+
+    def pool(d, carry):
+        rows = jnp.concatenate([received[o, d] for o in range(n_table)], axis=0)
+        values[...] = contract(counts[d], rows, 0, 0)
+        at = pl.ds(pl.multiple_of(d * samples, samples), samples)
+        for j in range(feats):
+            pooled[j, at, :] = values[pl.ds(j, samples, stride=pad), :].astype(BF16)
+        return carry
+
+    lax.fori_loop(0, n_table, pool, 0)
     to_scalar.wait()
     own_cot.wait()
     own_tiles.wait()
@@ -301,15 +333,15 @@
         lax.fori_loop(
             0, chunks, lambda chunk, carry, distance=distance: (arrive(chunk, distance), carry)[1], 0
         )
-    for copy in second:
-        copy.wait_recv()
 
     def work(chunk, carry):
         arrive(chunk, lines - 1)
         for line in range(lines):
             landed(chunk, 2 * line + 1 - core)
-        for b in range(step):
-            n = chunk * step + b
+        blocks = [chunk * step + b for b in range(step)]
+        weights = [w[n].reshape(per_block * emb, emb) for n in blocks]
+        pres = []
+        for b, n in enumerate(blocks):
             picked = jnp.concatenate(
                 [
                     pooled[plan_s[plan.shape[0] - 8 + i, me * col_blocks + n]]
@@ -317,14 +349,16 @@
                 ],
                 axis=1,
             )
-            weights = w[n].reshape(per_block * emb, emb)
-            pre = contract(picked, weights, 1, 0)
+            pres.append(contract(picked, weights[b], 1, 0))
+        grads = []
+        for n, pre in zip(blocks, pres):
             sig = jax.nn.sigmoid(pre)
             columns = pl.ds(pl.multiple_of(n * emb, emb), emb)
             act[:, columns] = (pre * sig).astype(BF16)
             up = cot[:, columns].astype(F32)
-            grad = (up * sig * (1.0 + pre * (1.0 - sig))).astype(BF16)
-            back_rows = contract(grad, weights, 1, 1)
+            grads.append((up * sig * (1.0 + pre * (1.0 - sig))).astype(BF16))
+        for b in range(step):
+            back_rows = contract(grads[b], weights[b], 1, 1)
             for i in range(per_block):
                 products[b, i] = back_rows[:, i * emb : (i + 1) * emb]
 
@@ -332,44 +366,36 @@
             value = products[0, plan_s[j, me * col_blocks + chunk * step]]
             for b in range(1, step):
                 value = value + products[b, plan_s[j, me * col_blocks + chunk * step + b]]
-            total[j] = jnp.where(chunk == 0, value, total[j] + value)
+            at = pl.ds(j, group, stride=pad)
+            spread[at, :] = spread[at, :] + value
             return c
 
         lax.fori_loop(0, feats, add, 0, unroll=2)
         return carry
 
-    total[...] = jnp.zeros(total.shape, F32)
     lax.fori_loop(0, chunks, work, 0)
     act_out = pltpu.make_async_copy(act, act_ref.at[0], local_sem.at[3])
     act_out.start()
 
-    part[...] = total[...].astype(BF16)
-    third = exchange(
-        2,
-        lambda peer: part.at[:, pl.ds(pl.multiple_of(peer * samples, samples), samples), :],
-        parts_in.at[me],
-    )
-    parts_in[me] = part[:, at_me, :]
-    spread[...] = jnp.zeros(spread.shape, F32)
+    partial = spread[...].astype(BF16)
+    for d in range(n_table):
+        rows = partial[d * samples * pad : (d + 1) * samples * pad]
+        slot_grads = contract(counts[d], rows, 1, 0).astype(BF16)
+        for o in range(n_table):
+            back[o, d] = slot_grads[o * slot_cap : (o + 1) * slot_cap]
+    third = exchange(2, lambda peer: back.at[peer], back_in.at[me])
+    back_in[me] = back[me]
     for copy in third:
         copy.wait_recv()
-    for j in range(feats):
-        value = parts_in[0, j].astype(F32)
-        for d in range(1, n_table):
-            value = value + parts_in[d, j].astype(F32)
-        spread[pl.ds(j, samples, stride=pad), :] = value
-    grads = spread[...]
-    high = grads.astype(BF16)
-    low = (grads - high.astype(F32)).astype(BF16)
-    slot_grads = contract(counts[...], high, 1, 0) + contract(counts[...], low, 1, 0)
-    back[...] = slot_grads.astype(BF16).reshape(n_table, slot_cap, emb)
-    fourth = exchange(3, lambda peer: back.at[peer], back_in.at[me])
-    back_in[me] = back[me]
-    for copy in fourth:
-        copy.wait_recv()
-    rows_ref[0] = contract(pick[...], back_in[...].reshape(slots, emb), 1, 0)
-
-    for copies in (first, second, third, fourth):
+    summed = back_in[0].astype(F32)
+    for t in range(1, n_table):
+        summed = summed + back_in[t].astype(F32)
+    summed = summed.reshape(slots, emb)
+    high = summed.astype(BF16)
+    low = (summed - high.astype(F32)).astype(BF16)
+    rows_ref[0] = contract(pick[...], high, 1, 0) + contract(pick[...], low, 1, 0)
+
+    for copies in (first, second, third):
         for copy in copies:
             copy.wait_send()
 
@@ -403,39 +429,43 @@
     per_row = 128 // pad
     plan_rows = pad + 8
     vmem, anywhere = pl.BlockSpec(memory_space=pltpu.VMEM), pl.BlockSpec(memory_space=pl.ANY)
+    hbm = pl.BlockSpec(memory_space=pltpu.HBM)
+    bags = jnp.swapaxes(bag_slots, 2, 3)
     return pl.pallas_call(
         functools.partial(body, n_table, n_fsdp, chunks),
         out_shape=(
             jax.ShapeDtypeStruct((1, group, col_blocks * emb), BF16),
             jax.ShapeDtypeStruct((1, row_count, emb), F32),
         ),
-        in_specs=[vmem, vmem, vmem, vmem, anywhere, anywhere],
+        in_specs=[hbm] * 6,
         out_specs=(anywhere, vmem),
         scratch_shapes=[
+            pltpu.VMEM(table_rows.shape, BF16),
+            pltpu.VMEM(requests.shape, jnp.int32),
+            pltpu.VMEM(bags.shape, jnp.int32),
+            pltpu.VMEM(pattern.shape[::-1], jnp.int32),
             pltpu.VMEM((col_blocks, per_block, tile_rows * n_fsdp, emb), BF16),
             pltpu.VMEM((group, col_blocks * emb), BF16),
             pltpu.VMEM((group, col_blocks * emb), BF16),
             pltpu.VMEM((1, slots), jnp.int32),
-            pltpu.VMEM((samples // per_row, depth, per_row * pad), jnp.int32),
+            pltpu.VMEM((n_table, samples // per_row, depth, per_row * pad), jnp.int32),
             pltpu.VMEM((row_count, slots), BF16),
-            pltpu.VMEM((slots, samples * pad), BF16),
-            pltpu.VMEM((n_table, slot_cap, emb), BF16),
-            pltpu.VMEM((n_table, slot_cap, emb), BF16),
+            pltpu.VMEM((n_table, slots, samples * pad), BF16),
+            pltpu.VMEM((n_table, n_table, slot_cap, emb), BF16),
             pltpu.VMEM((samples * pad, emb), F32),
+            pltpu.VMEM((group * pad, emb), F32),
             pltpu.VMEM((feats, group, emb), BF16),
             pltpu.VMEM((col_blocks // chunks, per_block + 1, group, emb), F32),
-            pltpu.VMEM((feats, group, emb), F32),
-            pltpu.VMEM((feats, group, emb), BF16),
-            pltpu.VMEM((n_table, feats, samples, emb), BF16),
-            pltpu.VMEM((n_table, slot_cap, emb), BF16),
-            pltpu.VMEM((n_table, slot_cap, emb), BF16),
+            pltpu.VMEM((n_table, n_table, slot_cap, emb), BF16),
+            pltpu.VMEM((n_table, n_table, slot_cap, emb), BF16),
             pltpu.VMEM((plan_rows, 128), jnp.int32),
             pltpu.SMEM((plan_rows, 128), jnp.int32),
             pltpu.SemaphoreType.DMA((4,)),
+            pltpu.SemaphoreType.DMA((4,)),
             pltpu.SemaphoreType.DMA((3, chunks, lines)),
             pltpu.SemaphoreType.DMA((chunks, n_fsdp)),
-            pltpu.SemaphoreType.DMA((4, n_table)),
-            pltpu.SemaphoreType.DMA((4, n_table)),
+            pltpu.SemaphoreType.DMA((3, n_table)),
+            pltpu.SemaphoreType.DMA((3, n_table)),
         ],
         compiler_params=pltpu.CompilerParams(
             collective_id=0, has_side_effects=True, vmem_limit_bytes=VMEM_LIMIT
@@ -443,7 +473,7 @@
     )(
         table_rows,
         requests,
-        jnp.swapaxes(bag_slots, 2, 3),
+        bags,
         pattern.T,
         tiles,
         cotangent,

time: 58.4 us -> 50.7 us (0.87)
  local copies, waits for them, and re-layouts: 6.4 us -> 2.42 us
  Pallas kernels: 51 us -> 47.5 us
    unnamed x14 -> x4, local copies, waits for them, and re-layouts: 6.4 us -> 2.42 us
    pallas_call x1, Pallas kernels: 51 us -> 47.5 us  [fused(): pl.pallas_call(functools.partial(body, n_table, n_fsdp, chunks), out_shap...]
where the time goes in v2:
time: 50.7 us; the launch traced here: 50.5 us
  Pallas kernels  47.5 us (94%)
  local copies, waits for them, and re-layouts  2.42 us (5%)
  between operations  0.65 us (1%)
    pallas_call x1, Pallas kernels, fused(): pl.pallas_call(functools.partial(body, n_table, n_fsdp, chunks), out_shap...  47.5 us
    unnamed x4, local copies, waits for them, and re-layouts  2.42 us

profile of v2, /device:TPU:0, one launch (start us, length us, event | category | flops | bytes accessed | tf_op | source)
XLA Modules:
  0.0 50.5 jit_solution(14531654896123498051)
XLA Ops:
  0.6 47.5 %shard_map.77 = (bf16[1,64,2048]{2,1,0:T(8,128)(2,1)}, f32[1,512,128]{2,1,0:T(8,128)}) custom-call(bf16[1,512,128]{2,1,0:T(8,128)(2,1)} %table_in.1, s32[1,1,4,32]{3,2,1,0:T(4,128)} %req_in.1, s32[1,16,4,26]{3,2,1,0:T(4,128)} %bitcast.2, s32[7,64]{1,0:T(8,128)} %bitcast.3, bf16[16,7,16,128]{3,2,1,0:T(8,128)(2,1)} %tiles_ref.1, bf16[1,64,2048]{2,1,0:T(8,128)(2,1)} %cot_ref.1), custom_call_target="tpu_custom_call" | custom-call | tf_op jit(solution)/shard_map/pallas_call | solution.py:434
  48.1 0.0 copy-start
  48.1 1.7 %copy.10 = bf16[1,64,2048]{2,1,0:T(8,128)(2,1)} copy(bf16[1,64,2048]{2,1,0:T(8,128)(2,1)} %get-tuple-element.4) | data formatting | bytes 524288
  49.8 0.0 copy-done
  49.8 0.7 %copy.11 = f32[1,512,128]{2,1,0:T(8,128)} copy(f32[1,512,128]{2,1,0:T(8,128)S(1)} %copy-done) | data formatting | bytes 524288
Async XLA Ops:
  48.1 1.7 %copy-start = (f32[1,512,128]{2,1,0:T(8,128)S(1)}, f32[1,512,128]{2,1,0:T(8,128)}, u32[]{:S(2)}) copy-start(f32[1,512,128]{2,1,0:T(8,128)} %get-tuple-element.5) | copy-start | bytes 786436

commit v3 on v2

--- a/solution.py
+++ b/solution.py
@@ -12,7 +12,7 @@
 BF16 = jnp.bfloat16
 TILE_ROWS = 16
 VMEM_LIMIT = 64 * 1024 * 1024
-CHUNKS = 4
+CUTS = (0, 0.5, 1)
 
 
 def local(table_rows, requests, bag_slots, pattern, tiles, cotangent):
@@ -90,7 +90,7 @@
 def body(
     n_table,
     n_fsdp,
-    chunks,
+    starts,
     table_in,
     req_in,
     bag_in,
@@ -108,11 +108,11 @@
     act,
     req_row,
     bag_rows,
+    bag_slots,
     pick,
     counts,
     received,
-    values,
-    spread,
+    total,
     pooled,
     products,
     back,
@@ -127,14 +127,14 @@
     t_recv,
 ):
     col_blocks, per_block, tile_rows, emb = tiles_ref.shape
-    step = col_blocks // chunks
+    chunks = len(starts) - 1
     lines = n_fsdp // 2
     samples, depth, feats = bag_ref.shape[1:]
     slot_cap = req_ref.shape[3]
     slots = n_table * slot_cap
     group = cot_ref.shape[1]
     row_count = table_ref.shape[1]
-    pad = bag_rows.shape[3] // (samples // bag_rows.shape[1])
+    pad = bag_rows.shape[2] // (samples // bag_rows.shape[0])
 
     me = lax.axis_index("table")
     mine = lax.axis_index("fsdp")
@@ -183,11 +183,11 @@
 
     def slot(chunk, source):
         at = pl.multiple_of(source * tile_rows, tile_rows)
-        return w.at[pl.ds(chunk * step, step), :, pl.ds(at, tile_rows), :]
+        return w.at[starts[chunk] : starts[chunk + 1], :, pl.ds(at, tile_rows), :]
 
     def hop(way, chunk, line, target, own=False):
         source = 2 * line + core
-        src = tiles_ref.at[pl.ds(chunk * step, step)] if own else slot(chunk, source)
+        src = tiles_ref.at[starts[chunk] : starts[chunk + 1]] if own else slot(chunk, source)
         return pltpu.make_async_remote_copy(
             src_ref=src,
             dst_ref=slot(chunk, source),
@@ -218,13 +218,15 @@
 
         return carry
 
-    lax.fori_loop(0, chunks, send_own, 0)
+    for chunk in range(chunks):
+        send_own(chunk, 0)
 
     def send_own_core(chunk, carry):
         hop(2, chunk, z, sibling, True).start()
         return carry
 
-    lax.fori_loop(0, chunks, send_own_core, 0)
+    for chunk in range(chunks):
+        send_own_core(chunk, 0)
 
     def exchange(phase, source_of, target):
         copies = []
@@ -255,14 +257,24 @@
     first = exchange(0, lambda peer: received.at[me], received.at[me])
     loads[2].wait()
     loads[3].wait()
-    quads = bag_rows.shape[1]
+    quads = bag_rows.shape[0]
     per_row = samples // quads
     width = per_row * pad
-    bag_rows[me] = jnp.full(bag_rows.shape[1:], -1, jnp.int32)
+    bag_rows[...] = jnp.full(bag_rows.shape, -1, jnp.int32)
     for s in range(samples):
         at = (s % per_row) * pad
-        bag_rows[me, s // per_row, :, at : at + feats] = bag_ref[0, s]
-    second = exchange(1, lambda peer: bag_rows.at[me], bag_rows.at[me])
+        bag_rows[s // per_row, 0:depth, at : at + feats] = bag_ref[0, s]
+    by_sample = jnp.concatenate([bag_rows[g] for g in range(quads)], axis=1)
+    total_width = quads * width
+    source = lax.broadcasted_iota(jnp.int32, (total_width, total_width), 0)
+    target = lax.broadcasted_iota(jnp.int32, (total_width, total_width), 1)
+    moves = (target % samples) * pad + target // samples == source
+    by_feature = contract(
+        by_sample.astype(F32).astype(BF16), jnp.where(moves, 1.0, 0.0).astype(BF16), 1, 0
+    )
+    used = lax.broadcasted_iota(jnp.int32, by_feature.shape, 1) < feats * samples
+    bag_slots[me] = jnp.where(used, by_feature, -1.0)
+    second = exchange(1, lambda peer: bag_slots.at[me], bag_slots.at[me])
 
     plan[...] = jnp.zeros(plan.shape, jnp.int32)
     feat_ids = lax.broadcasted_iota(jnp.int32, (plan.shape[0] - 8, pattern_ref.shape[1]), 0)
@@ -275,16 +287,16 @@
     ]
     to_scalar = pltpu.make_async_copy(plan, plan_s, local_sem.at[2])
     to_scalar.start()
-    products[:, per_block] = jnp.zeros((step, group, emb), F32)
-    spread[...] = jnp.zeros(spread.shape, F32)
+    products[:, per_block] = jnp.zeros((products.shape[0], group, emb), F32)
+    total[...] = jnp.zeros(total.shape, F32)
 
     for copy in second:
         copy.wait_recv()
-    slot_ids = lax.broadcasted_iota(jnp.int32, (slots, width), 0)
+    slot_ids = lax.broadcasted_iota(jnp.int32, (slots, width), 0).astype(F32)
 
     def count(d, carry):
         for g in range(quads):
-            rows = bag_rows[d, g]
+            rows = bag_slots[d, :, g * width : (g + 1) * width]
             found = jnp.zeros((slots, width), F32)
             for k in range(depth):
                 found = found + jnp.where(slot_ids == rows[k : k + 1, :], 1.0, 0.0)
@@ -297,10 +309,9 @@
 
     def pool(d, carry):
         rows = jnp.concatenate([received[o, d] for o in range(n_table)], axis=0)
-        values[...] = contract(counts[d], rows, 0, 0)
+        values = contract(counts[d], rows, 0, 0).astype(BF16)
         at = pl.ds(pl.multiple_of(d * samples, samples), samples)
-        for j in range(feats):
-            pooled[j, at, :] = values[pl.ds(j, samples, stride=pad), :].astype(BF16)
+        pooled[:, at, :] = values[: feats * samples].reshape(feats, samples, emb)
         return carry
 
     lax.fori_loop(0, n_table, pool, 0)
@@ -330,15 +341,15 @@
             hop(2, chunk, z + distance, sibling).start()
 
     for distance in range(1, lines - 1):
-        lax.fori_loop(
-            0, chunks, lambda chunk, carry, distance=distance: (arrive(chunk, distance), carry)[1], 0
-        )
+        for chunk in range(chunks):
+            arrive(chunk, distance)
 
     def work(chunk, carry):
         arrive(chunk, lines - 1)
         for line in range(lines):
             landed(chunk, 2 * line + 1 - core)
-        blocks = [chunk * step + b for b in range(step)]
+        blocks = range(starts[chunk], starts[chunk + 1])
+        step = len(blocks)
         weights = [w[n].reshape(per_block * emb, emb) for n in blocks]
         pres = []
         for b, n in enumerate(blocks):
@@ -353,7 +364,7 @@
         grads = []
         for n, pre in zip(blocks, pres):
             sig = jax.nn.sigmoid(pre)
-            columns = pl.ds(pl.multiple_of(n * emb, emb), emb)
+            columns = slice(n * emb, (n + 1) * emb)
             act[:, columns] = (pre * sig).astype(BF16)
             up = cot[:, columns].astype(F32)
             grads.append((up * sig * (1.0 + pre * (1.0 - sig))).astype(BF16))
@@ -363,24 +374,24 @@
                 products[b, i] = back_rows[:, i * emb : (i + 1) * emb]
 
         def add(j, c):
-            value = products[0, plan_s[j, me * col_blocks + chunk * step]]
+            value = products[0, plan_s[j, me * col_blocks + blocks[0]]]
             for b in range(1, step):
-                value = value + products[b, plan_s[j, me * col_blocks + chunk * step + b]]
-            at = pl.ds(j, group, stride=pad)
-            spread[at, :] = spread[at, :] + value
+                value = value + products[b, plan_s[j, me * col_blocks + blocks[b]]]
+            total[j] = total[j] + value
             return c
 
-        lax.fori_loop(0, feats, add, 0, unroll=2)
+        lax.fori_loop(0, feats, add, 0, unroll=True)
         return carry
 
-    lax.fori_loop(0, chunks, work, 0)
+    for chunk in range(chunks):
+        work(chunk, 0)
     act_out = pltpu.make_async_copy(act, act_ref.at[0], local_sem.at[3])
     act_out.start()
 
-    partial = spread[...].astype(BF16)
     for d in range(n_table):
-        rows = partial[d * samples * pad : (d + 1) * samples * pad]
-        slot_grads = contract(counts[d], rows, 1, 0).astype(BF16)
+        rows = total[:, d * samples : (d + 1) * samples, :].astype(BF16)
+        rows = rows.reshape(feats * samples, emb)
+        slot_grads = contract(counts[d, :, 0 : feats * samples], rows, 1, 0).astype(BF16)
         for o in range(n_table):
             back[o, d] = slot_grads[o * slot_cap : (o + 1) * slot_cap]
     third = exchange(2, lambda peer: back.at[peer], back_in.at[me])
@@ -413,11 +424,12 @@
 
         return carry
 
-    lax.fori_loop(0, chunks, sent_all, 0)
+    for chunk in range(chunks):
+        sent_all(chunk, 0)
     act_out.wait()
 
 
-def fused(n_table, n_fsdp, chunks, table_rows, requests, bag_slots, pattern, tiles, cotangent):
+def fused(n_table, n_fsdp, table_rows, requests, bag_slots, pattern, tiles, cotangent):
     col_blocks, per_block, tile_rows, emb = tiles.shape
     group = cotangent.shape[1]
     row_count = table_rows.shape[1]
@@ -425,6 +437,9 @@
     slot_cap = requests.shape[3]
     slots = n_table * slot_cap
     lines = n_fsdp // 2
+    starts = tuple(round(col_blocks * cut) for cut in CUTS)
+    longest = max(b - a for a, b in zip(starts, starts[1:]))
+    chunks = len(starts) - 1
     pad = 32
     per_row = 128 // pad
     plan_rows = pad + 8
@@ -432,7 +447,7 @@
     hbm = pl.BlockSpec(memory_space=pltpu.HBM)
     bags = jnp.swapaxes(bag_slots, 2, 3)
     return pl.pallas_call(
-        functools.partial(body, n_table, n_fsdp, chunks),
+        functools.partial(body, n_table, n_fsdp, starts),
         out_shape=(
             jax.ShapeDtypeStruct((1, group, col_blocks * emb), BF16),
             jax.ShapeDtypeStruct((1, row_count, emb), F32),
@@ -448,14 +463,14 @@
             pltpu.VMEM((group, col_blocks * emb), BF16),
             pltpu.VMEM((group, col_blocks * emb), BF16),
             pltpu.VMEM((1, slots), jnp.int32),
-            pltpu.VMEM((n_table, samples // per_row, depth, per_row * pad), jnp.int32),
+            pltpu.VMEM((samples // per_row, 8, per_row * pad), jnp.int32),
+            pltpu.VMEM((n_table, 8, samples * pad), F32),
             pltpu.VMEM((row_count, slots), BF16),
             pltpu.VMEM((n_table, slots, samples * pad), BF16),
             pltpu.VMEM((n_table, n_table, slot_cap, emb), BF16),
-            pltpu.VMEM((samples * pad, emb), F32),
-            pltpu.VMEM((group * pad, emb), F32),
+            pltpu.VMEM((feats, group, emb), F32),
             pltpu.VMEM((feats, group, emb), BF16),
-            pltpu.VMEM((col_blocks // chunks, per_block + 1, group, emb), F32),
+            pltpu.VMEM((longest, per_block + 1, group, emb), F32),
             pltpu.VMEM((n_table, n_table, slot_cap, emb), BF16),
             pltpu.VMEM((n_table, n_table, slot_cap, emb), BF16),
             pltpu.VMEM((plan_rows, 128), jnp.int32),
@@ -501,11 +516,12 @@
             and emb == 128
             and n_table * requests.shape[3] == 128
             and feats <= 32
+            and bag_slots.shape[3] <= 8
             and n_fsdp % 2 == 0
-            and col_blocks % CHUNKS == 0
+            and col_blocks % 16 == 0
         )
         if whole:
-            run = functools.partial(fused, n_table, n_fsdp, CHUNKS)
+            run = functools.partial(fused, n_table, n_fsdp)
         else:
             run = local
         return run(table_rows, requests, bag_slots, pattern, tiles, cotangent)

time: 50.7 us -> 46.5 us (0.917)
  Pallas kernels: 47.5 us -> 43.2 us
    pallas_call x1, Pallas kernels: 47.5 us -> 43.2 us  [fused(): pl.pallas_call(functools.partial(body, n_table, n_fsdp, starts), out_shap...]
where the time goes in v3:
time: 46.5 us; the launch traced here: 46.3 us
  Pallas kernels  43.2 us (93%)
  local copies, waits for them, and re-layouts  2.42 us (5%)
  between operations  0.65 us (1%)
    pallas_call x1, Pallas kernels, fused(): pl.pallas_call(functools.partial(body, n_table, n_fsdp, starts), out_shap...  43.2 us
    unnamed x4, local copies, waits for them, and re-layouts  2.42 us

profile of v3, /device:TPU:0, one launch (start us, length us, event | category | flops | bytes accessed | tf_op | source)
XLA Modules:
  0.0 46.3 jit_solution(9868276174940301960)
XLA Ops:
  0.6 43.2 %shard_map.77 = (bf16[1,64,2048]{2,1,0:T(8,128)(2,1)}, f32[1,512,128]{2,1,0:T(8,128)}) custom-call(bf16[1,512,128]{2,1,0:T(8,128)(2,1)} %table_in.1, s32[1,1,4,32]{3,2,1,0:T(4,128)} %req_in.1, s32[1,16,4,26]{3,2,1,0:T(4,128)} %bitcast.2, s32[7,64]{1,0:T(8,128)} %bitcast.3, bf16[16,7,16,128]{3,2,1,0:T(8,128)(2,1)} %tiles_ref.1, bf16[1,64,2048]{2,1,0:T(8,128)(2,1)} %cot_ref.1), custom_call_target="tpu_custom_call" | custom-call | tf_op jit(solution)/shard_map/pallas_call | solution.py:449
  43.8 0.0 copy-start
  43.9 1.7 %copy.10 = bf16[1,64,2048]{2,1,0:T(8,128)(2,1)} copy(bf16[1,64,2048]{2,1,0:T(8,128)(2,1)} %get-tuple-element.4) | data formatting | bytes 524288
  45.6 0.0 copy-done
  45.6 0.7 %copy.11 = f32[1,512,128]{2,1,0:T(8,128)} copy(f32[1,512,128]{2,1,0:T(8,128)S(1)} %copy-done) | data formatting | bytes 524288
Async XLA Ops:
  43.8 1.7 %copy-start = (f32[1,512,128]{2,1,0:T(8,128)S(1)}, f32[1,512,128]{2,1,0:T(8,128)}, u32[]{:S(2)}) copy-start(f32[1,512,128]{2,1,0:T(8,128)} %get-tuple-element.5) | copy-start | bytes 786436

commit v4 on v3

--- a/solution.py
+++ b/solution.py
@@ -176,8 +176,10 @@
         local_sem.at[0],
     )
     own_cot = pltpu.make_async_copy(cot_ref.at[0], cot, local_sem.at[1])
+    own_tiles.start()
     own_cot.start()
 
+    own_tiles.wait()
     neighbours = jnp.where(z > 0, 1, 0) + jnp.where(z < lines - 1, 1, 0)
     pl.semaphore_wait(barrier, n_table + neighbours)
 
@@ -187,7 +189,7 @@
 
     def hop(way, chunk, line, target, own=False):
         source = 2 * line + core
-        src = tiles_ref.at[starts[chunk] : starts[chunk + 1]] if own else slot(chunk, source)
+        src = slot(chunk, source)
         return pltpu.make_async_remote_copy(
             src_ref=src,
             dst_ref=slot(chunk, source),
@@ -225,8 +227,6 @@
         hop(2, chunk, z, sibling, True).start()
         return carry
 
-    for chunk in range(chunks):
-        send_own_core(chunk, 0)
 
     def exchange(phase, source_of, target):
         copies = []
@@ -244,7 +244,6 @@
             copies.append(copy)
         return copies
 
-    own_tiles.start()
     loads[0].wait()
     for d in range(n_table):
         req_row[:, d * slot_cap : (d + 1) * slot_cap] = req_ref[0, 0, d : d + 1, :]
@@ -276,6 +275,8 @@
     bag_slots[me] = jnp.where(used, by_feature, -1.0)
     second = exchange(1, lambda peer: bag_slots.at[me], bag_slots.at[me])
 
+    for chunk in range(chunks):
+        send_own_core(chunk, 0)
     plan[...] = jnp.zeros(plan.shape, jnp.int32)
     feat_ids = lax.broadcasted_iota(jnp.int32, (plan.shape[0] - 8, pattern_ref.shape[1]), 0)
     inverse = jnp.full(feat_ids.shape, per_block, jnp.int32)
@@ -314,10 +315,8 @@
         pooled[:, at, :] = values[: feats * samples].reshape(feats, samples, emb)
         return carry
 
-    lax.fori_loop(0, n_table, pool, 0)
     to_scalar.wait()
     own_cot.wait()
-    own_tiles.wait()
 
     def arrive(chunk, distance):
         @pl.when(z >= distance)
@@ -343,6 +342,8 @@
     for distance in range(1, lines - 1):
         for chunk in range(chunks):
             arrive(chunk, distance)
+
+    lax.fori_loop(0, n_table, pool, 0)
 
     def work(chunk, carry):
         arrive(chunk, lines - 1)

time: 46.5 us -> 46.2 us (level)
  no operation moved by 1% of the time
where the time goes in v4:
time: 46.2 us; the launch traced here: 46 us
  Pallas kernels  43 us (93%)
  local copies, waits for them, and re-layouts  2.42 us (5%)
  between operations  0.65 us (1%)
    pallas_call x1, Pallas kernels, fused(): pl.pallas_call(functools.partial(body, n_table, n_fsdp, starts), out_shap...  43 us
    unnamed x4, local copies, waits for them, and re-layouts  2.42 us

profile of v4, /device:TPU:0, one launch (start us, length us, event | category | flops | bytes accessed | tf_op | source)
XLA Modules:
  0.0 46.0 jit_solution(8426238017908971774)
XLA Ops:
  0.6 43.0 %shard_map.77 = (bf16[1,64,2048]{2,1,0:T(8,128)(2,1)}, f32[1,512,128]{2,1,0:T(8,128)}) custom-call(bf16[1,512,128]{2,1,0:T(8,128)(2,1)} %table_in.1, s32[1,1,4,32]{3,2,1,0:T(4,128)} %req_in.1, s32[1,16,4,26]{3,2,1,0:T(4,128)} %bitcast.2, s32[7,64]{1,0:T(8,128)} %bitcast.3, bf16[16,7,16,128]{3,2,1,0:T(8,128)(2,1)} %tiles_ref.1, bf16[1,64,2048]{2,1,0:T(8,128)(2,1)} %cot_ref.1), custom_call_target="tpu_custom_call" | custom-call | tf_op jit(solution)/shard_map/pallas_call | solution.py:450
  43.6 0.0 copy-start
  43.6 1.7 %copy.10 = bf16[1,64,2048]{2,1,0:T(8,128)(2,1)} copy(bf16[1,64,2048]{2,1,0:T(8,128)(2,1)} %get-tuple-element.4) | data formatting | bytes 524288
  45.3 0.0 copy-done
  45.3 0.7 %copy.11 = f32[1,512,128]{2,1,0:T(8,128)} copy(f32[1,512,128]{2,1,0:T(8,128)S(1)} %copy-done) | data formatting | bytes 524288
Async XLA Ops:
  43.6 1.7 %copy-start = (f32[1,512,128]{2,1,0:T(8,128)S(1)}, f32[1,512,128]{2,1,0:T(8,128)}, u32[]{:S(2)}) copy-start(f32[1,512,128]{2,1,0:T(8,128)} %get-tuple-element.5) | copy-start | bytes 786436
